TPU v7x, 768 devices: a whole 4x8x12 slice. The times are simulated.
768 devices in a mesh: dp: 96 (over z, x, y_hi), group: 8 (over y_lo, core).
Axes of the slice: x: 4, y: 8 (y_hi: 2, y_lo: 4; y = y_hi * 4 + y_lo), z: 12, core: 2. Of those that a mesh axis runs over, the one named last changes fastest.
Arguments:
- image: bfloat16 [294912, 1152], P(('dp', 'group')), may hold values from -0.1875 to 0.1875
- text: bfloat16 [294912, 1152], P(('dp', 'group')), may hold values from -0.1875 to 0.1875
- caption_index: int32 [768, 384], P(('dp', 'group')), may hold values from 0 to 383, each once within a row
- log_scale: float32 [], replicated, may hold values from 1.5 to 3
- bias: float32 [], replicated, may hold values from -4 to -1
Outputs:
- grad_image: bfloat16 [294912, 1152], P(('dp', 'group'))
- grad_text: bfloat16 [294912, 1152], P(('dp', 'group'))
- row_loss: float32 [294912], P(('dp', 'group'))
Inputs may be any that keep to these rules, and one draw needn't show every extreme that they name: Each row of caption_index holds every number below 384 exactly once.
All inputs are finite; a program needn't handle non-finite values.
Results may differ from a plain program's by a relative error of at most 0.0095.
Values may be sent and summed in bfloat16 or wider, within the bound.
A program may use at most 32 MiB of HBM per device.

v0:
```python
import jax
import jax.numpy as jnp
from jax import lax
from jax.sharding import PartitionSpec as P


def passed_along(value, axis, steps):
    count = lax.axis_size(axis)
    pairs = [(source, (source + steps) % count) for source in range(count)]
    return lax.ppermute(value, axis, pairs)


def tile_terms(image_rows, text_rows, scale, bias, positive):
    logits = scale * jnp.dot(image_rows, text_rows.T, preferred_element_type=jnp.float32) + bias
    signs = jnp.where(positive, jnp.float32(1.0), jnp.float32(-1.0))
    terms = jax.nn.softplus(-signs * logits)
    coef = (jax.nn.sigmoid(logits) - positive.astype(jnp.float32)).astype(jnp.bfloat16)
    return (jnp.sum(terms, axis=1), coef)


def text_part(coef, image_rows, scale):
    return (scale * jnp.dot(coef.T, image_rows, preferred_element_type=jnp.float32)).astype(
        jnp.bfloat16
    )


def body(image, text, caption_index, log_scale, bias):
    rows = image.shape[0]
    scale = jnp.exp(log_scale)
    distance = lax.axis_size(("dp", "group")) // 2 + 1
    columns = jnp.arange(rows, dtype=jnp.int32)
    positive = caption_index[0][:, None] == columns[None, :]
    nothing = jnp.zeros((rows, rows), dtype=bool)
    loss_own, coef_own = tile_terms(image, text, scale, bias, positive)
    near_text = passed_along(text, "dp", 1)
    loss_near, coef_near = tile_terms(image, near_text, scale, bias, nothing)
    far_text = passed_along(text, ("dp", "group"), distance)
    loss_far, coef_far = tile_terms(image, far_text, scale, bias, nothing)
    image_near = (scale * jnp.dot(coef_near, near_text, preferred_element_type=jnp.float32)).astype(
        jnp.bfloat16
    )
    image_far = (scale * jnp.dot(coef_far, far_text, preferred_element_type=jnp.float32)).astype(
        jnp.bfloat16
    )
    grad_image = scale * jnp.dot(coef_own, text, preferred_element_type=jnp.float32)
    grad_image = (
        grad_image + image_near.astype(jnp.float32) + image_far.astype(jnp.float32)
    ).astype(jnp.bfloat16)
    row_loss = (loss_own + loss_near + loss_far) / jnp.float32(3 * rows)
    text_near = passed_along(text_part(coef_near, image, scale), "dp", -1)
    text_far = passed_along(text_part(coef_far, image, scale), ("dp", "group"), -distance)
    grad_text = scale * jnp.dot(coef_own.T, image, preferred_element_type=jnp.float32)
    grad_text = (grad_text + text_near.astype(jnp.float32) + text_far.astype(jnp.float32)).astype(
        jnp.bfloat16
    )
    return (grad_image, grad_text, row_loss)


def solution(mesh):
    return jax.shard_map(
        body,
        mesh=mesh,
        in_specs=(
            P(("dp", "group"), None),
            P(("dp", "group"), None),
            P(("dp", "group"), None),
            P(),
            P(),
        ),
        out_specs=(P(("dp", "group"), None), P(("dp", "group"), None), P(("dp", "group"))),
        check_vma=False,
    )
```

profile of v0, /device:TPU:400, one launch (start us, length us, event | category | flops | bytes accessed | tf_op | source)
XLA Modules:
  0.0 200.9 jit_solution(17260561351589405110)
XLA Ops:
  0.6 0.0 copy-start
  0.6 2.1 %collective-permute-start.1 = (bf16[384,1152]{1,0:T(8,128)(2,1)}, bf16[384,1152]{1,0:T(8,128)(2,1)S(1)}, u32[]{:S(2)}, u32[]{:S(2)}) collective-permute-start(bf16[384,1152]{1,0:T(8,128)(2,1)} %param.6), channel_id=1, source_target_pairs={{0,385},{1,386},{2,387},{3,388},{4,389},{5,390},{6,391},{7,392},{8... | collective-permute-start | bytes 2654216 | tf_op jit(solution)/shard_map/ppermute | solution.py:10
  2.7 5.9 %collective-permute-start = (bf16[384,1152]{1,0:T(8,128)(2,1)}, bf16[384,1152]{1,0:T(8,128)(2,1)S(1)}, u32[]{:S(2)}, u32[]{:S(2)}) collective-permute-start(bf16[384,1152]{1,0:T(8,128)(2,1)} %param.6), channel_id=1, source_target_pairs={{0,8},{8,16},{16,24},{24,32},{32,40},{40,48},{48,56},{56,64},{64,7... | collective-permute-start | bytes 2654216 | tf_op jit(solution)/shard_map/ppermute | solution.py:10
  10.0 0.7 reduce
  10.7 0.0 copy-done
  10.7 0.0 copy-start.1
  10.7 2.3 %fusion.12 = (f32[384]{0:T(512)S(1)}, f32[384,384]{0,1:T(8,128)S(1)}) fusion(s32[384]{0:T(512)S(1)} %reduce, f32[]{:T(128)S(6)} %copy.9, bf16[384,1152]{1,0:T(8,128)(2,1)S(1)} %copy-done, bf16[384,1152]{1,0:T(8,128)(2,1)} %param.6, f32[]{:T(128)S(6)} %exp.22), kind=kOutput, calls=%fused_computation.25 | convolution fusion | flops 341655168 | bytes 2362376 | tf_op jit(solution)/shard_map/dot_general | solution.py:14
  13.0 0.0 copy-done.1
  13.0 0.7 convolution_multiply_fusion.5
  13.7 55.2 %collective-permute-done.1 = bf16[384,1152]{1,0:T(8,128)(2,1)S(1)} collective-permute-done((bf16[384,1152]{1,0:T(8,128)(2,1)}, bf16[384,1152]{1,0:T(8,128)(2,1)S(1)}, u32[]{:S(2)}, u32[]{:S(2)}) %collective-permute-start.1) | collective-permute-done | bytes 884768 | tf_op jit(solution)/shard_map/ppermute | solution.py:10
  69.0 1.0 fusion.14
  69.9 0.6 fusion.3
  70.6 1.9 collective-permute-start.3
  72.5 97.7 %collective-permute-done = bf16[384,1152]{1,0:T(8,128)(2,1)S(1)} collective-permute-done((bf16[384,1152]{1,0:T(8,128)(2,1)}, bf16[384,1152]{1,0:T(8,128)(2,1)S(1)}, u32[]{:S(2)}, u32[]{:S(2)}) %collective-permute-start) | collective-permute-done | bytes 884768 | tf_op jit(solution)/shard_map/ppermute | solution.py:10
  170.2 1.0 fusion.13
  171.2 0.6 fusion.2
  171.8 1.9 collective-permute-start.2
  173.7 0.6 add_multiply_fusion
  174.3 0.7 fusion.8
  175.0 1.6 fusion.6
  176.7 0.0 collective-permute-done.3
  176.7 22.6 %collective-permute-done.2 = bf16[384,1152]{1,0:T(8,128)(2,1)S(1)} collective-permute-done((bf16[384,1152]{1,0:T(8,128)(2,1)S(1)}, bf16[384,1152]{1,0:T(8,128)(2,1)S(1)}, u32[]{:S(2)}, u32[]{:S(2)}) %collective-permute-start.2) | collective-permute-done | bytes 884768 | tf_op jit(solution)/shard_map/ppermute | solution.py:10
  199.3 1.6 add_convert_fusion
Async XLA Ops:
  0.6 10.1 %copy-start = (bf16[384,1152]{1,0:T(8,128)(2,1)S(1)}, bf16[384,1152]{1,0:T(8,128)(2,1)}, u32[]{:S(2)}) copy-start(bf16[384,1152]{1,0:T(8,128)(2,1)} %param.5) | copy-start | bytes 2654212
  0.6 68.3 %collective-permute-start.1 = (bf16[384,1152]{1,0:T(8,128)(2,1)}, bf16[384,1152]{1,0:T(8,128)(2,1)S(1)}, u32[]{:S(2)}, u32[]{:S(2)}) collective-permute-start(bf16[384,1152]{1,0:T(8,128)(2,1)} %param.6), channel_id=1, source_target_pairs={{0,385},{1,386},{2,387},{3,388},{4,389},{5,390},{6,391},{7,392},{8... | collective-permute-start | bytes 2654216 | tf_op jit(solution)/shard_map/ppermute | solution.py:10
  2.7 167.5 %collective-permute-start = (bf16[384,1152]{1,0:T(8,128)(2,1)}, bf16[384,1152]{1,0:T(8,128)(2,1)S(1)}, u32[]{:S(2)}, u32[]{:S(2)}) collective-permute-start(bf16[384,1152]{1,0:T(8,128)(2,1)} %param.6), channel_id=1, source_target_pairs={{0,8},{8,16},{16,24},{24,32},{32,40},{40,48},{48,56},{56,64},{64,7... | collective-permute-start | bytes 2654216 | tf_op jit(solution)/shard_map/ppermute | solution.py:10
  10.7 2.3 %copy-start.1 = (bf16[384,1152]{1,0:T(8,128)(2,1)S(1)}, bf16[384,1152]{1,0:T(8,128)(2,1)}, u32[]{:S(2)}) copy-start(bf16[384,1152]{1,0:T(8,128)(2,1)} %param.6) | copy-start | bytes 2654212
  70.6 106.1 %collective-permute-start.3 = (bf16[384,1152]{1,0:T(8,128)(2,1)S(1)}, bf16[384,1152]{1,0:T(8,128)(2,1)S(1)}, u32[]{:S(2)}, u32[]{:S(2)}) collective-permute-start(bf16[384,1152]{1,0:T(8,128)(2,1)S(1)} %fusion.3), channel_id=1, source_target_pairs={{0,383},{1,384},{2,385},{3,386},{4,387},{5,388},{6,389},{7,390},{8... | collective-permute-start | bytes 2654216 | tf_op jit(solution)/shard_map/ppermute | solution.py:10
  171.8 27.5 %collective-permute-start.2 = (bf16[384,1152]{1,0:T(8,128)(2,1)S(1)}, bf16[384,1152]{1,0:T(8,128)(2,1)S(1)}, u32[]{:S(2)}, u32[]{:S(2)}) collective-permute-start(bf16[384,1152]{1,0:T(8,128)(2,1)S(1)} %fusion.2), channel_id=1, source_target_pairs={{0,760},{8,0},{16,8},{24,16},{32,24},{40,32},{48,40},{56,48},{64,5... | collective-permute-start | bytes 2654216 | tf_op jit(solution)/shard_map/ppermute | solution.py:10
where the time goes:
time: 201 us
  waiting for transfers between devices  176 us (88%)
  starting transfers between devices  11.8 us (6%)
  matrix products  10.2 us (5%)
  between operations  2.05 us (1%)
    ppermute x4, waiting for transfers between devices, passed_along(): return lax.ppermute(value, axis, pairs)  176 us
    ppermute x4, starting transfers between devices, passed_along(): return lax.ppermute(value, axis, pairs)  11.8 us
    dot_general x3, matrix products, tile_terms(): jnp.dot(image_rows, text_rows.T, preferred_element_type=jnp.float32)  4.24 us
  transfers between devices with their start and end apart: 4, of which 3 were waited for; matrix products, arithmetic and copies ran while one was open for 5% of the time, Pallas kernels for 0%

commit v1 on v0

v1 whole, which is shorter than its diff:
```python
import functools

import jax
import jax.numpy as jnp
from jax import lax
from jax.experimental import pallas as pl
from jax.experimental.pallas import tpu as pltpu
from jax.sharding import PartitionSpec as P

MESH = pl.DeviceIdType.MESH
CHUNKS = 4


def dot_nt(a, b):
    return lax.dot_general(a, b, (((1,), (1,)), ((), ())), preferred_element_type=jnp.float32)


def dot_tn(a, b):
    return lax.dot_general(a, b, (((0,), (0,)), ((), ())), preferred_element_type=jnp.float32)


def halves(logits):
    small = jnp.exp(-jnp.abs(logits))
    loss = jnp.maximum(logits, 0.0) + jnp.log1p(small)
    chance = jnp.where(logits >= 0, 1.0, small) / (1.0 + small)
    return loss, chance


def kernel(
    groups, blocks,
    image, text, caption, log_scale, bias,
    grad_image, grad_text, row_loss,
    own_image, own_text, near_text, near_image, far_text, far_image, sum_image, sum_text,
    load_sem, send_sem, recv_sem,
):
    rows = image.shape[0]
    part = rows // CHUNKS
    me = lax.axis_index("dp") * groups + lax.axis_index("group")

    def device(step):
        at = lax.rem(me + step + blocks, blocks)
        return (at // groups, lax.rem(at, groups))

    far = blocks // 2 + 1
    flows = (
        (far_text, text, device(far)),
        (far_image, image, device(-far)),
        (near_text, text, device(groups)),
        (near_image, image, device(-groups)),
    )
    barrier = pltpu.get_barrier_semaphore()
    for _, _, peer in flows:
        pl.semaphore_signal(barrier, inc=1, device_id=peer, device_id_type=MESH)
    pl.semaphore_wait(barrier, len(flows))

    def copy(flow, k):
        target, source, peer = flows[flow]
        piece = pl.ds(pl.multiple_of(k * part, part), part)
        return pltpu.make_async_remote_copy(
            src_ref=source.at[piece],
            dst_ref=target.at[piece],
            send_sem=send_sem.at[flow, k],
            recv_sem=recv_sem.at[flow, k],
            device_id=peer,
            device_id_type=MESH,
        )

    for k in range(CHUNKS):
        for flow in range(len(flows)):
            copy(flow, k).start()

    loads = [
        pltpu.make_async_copy(image, own_image, load_sem.at[0]),
        pltpu.make_async_copy(text, own_text, load_sem.at[1]),
    ]
    for load in loads:
        load.start()
    for load in loads:
        load.wait()

    scale = jnp.exp(jnp.full((1, rows), log_scale[0], jnp.float32))
    shift = bias[0]

    row_loss[...] = jnp.zeros_like(row_loss)

    def own(k, _):
        piece = pl.ds(pl.multiple_of(k * part, part), part)
        texts = own_text[piece, :]
        logits = scale * dot_nt(texts, own_image[...]) + shift
        loss, chance = halves(logits)
        line = lax.broadcasted_iota(jnp.int32, (part, rows), 0) + k * part
        positive = line == caption[...]
        loss = loss - jnp.where(positive, logits, 0.0)
        coef = (chance - positive.astype(jnp.float32)).astype(jnp.bfloat16)
        row_loss[...] += jnp.sum(loss, axis=0, keepdims=True)
        sum_text[piece, :] = jnp.dot(coef, own_image[...], preferred_element_type=jnp.float32)
        add = dot_tn(coef, texts)

        @pl.when(k == 0)
        def _():
            sum_image[...] = add

        @pl.when(k > 0)
        def _():
            sum_image[...] += add

        return 0

    lax.fori_loop(0, CHUNKS, own, 0)

    def pair(flow_text, flow_image):
        def step(k, _):
            piece = pl.ds(pl.multiple_of(k * part, part), part)
            copy(flow_text, k).wait_recv()
            texts = flows[flow_text][0][piece, :]
            loss, chance = halves(scale * dot_nt(texts, own_image[...]) + shift)
            row_loss[...] += jnp.sum(loss, axis=0, keepdims=True)
            sum_image[...] += dot_tn(chance.astype(jnp.bfloat16), texts)
            copy(flow_image, k).wait_recv()
            images = flows[flow_image][0][piece, :]
            _, chance = halves(scale * dot_nt(images, own_text[...]) + shift)
            sum_text[...] += dot_tn(chance.astype(jnp.bfloat16), images)
            return 0

        lax.fori_loop(0, CHUNKS, step, 0)

    pair(2, 3)
    pair(0, 1)
    wide = jnp.exp(jnp.full((1, image.shape[1]), log_scale[0], jnp.float32))
    grad_image[...] = (wide * sum_image[...]).astype(grad_image.dtype)
    grad_text[...] = (wide * sum_text[...]).astype(grad_text.dtype)
    row_loss[...] = row_loss[...] / jnp.float32(3 * rows)

    def drain(k, _):
        for flow in range(len(flows)):
            copy(flow, k).wait_send()
        return 0

    lax.fori_loop(0, CHUNKS, drain, 0)


def solution(mesh):
    groups = mesh.shape["group"]
    blocks = mesh.shape["dp"] * groups

    def body(image, text, caption, log_scale, bias):
        rows, width = image.shape
        block = pltpu.VMEM((rows, width), jnp.bfloat16)
        total = pltpu.VMEM((rows, width), jnp.float32)
        vmem = pl.BlockSpec(memory_space=pltpu.VMEM)
        smem = pl.BlockSpec(memory_space=pltpu.SMEM)
        anywhere = pl.BlockSpec(memory_space=pl.ANY)
        grad_image, grad_text, row_loss = pl.pallas_call(
            functools.partial(kernel, groups, blocks),
            out_shape=(
                jax.ShapeDtypeStruct((rows, width), jnp.bfloat16),
                jax.ShapeDtypeStruct((rows, width), jnp.bfloat16),
                jax.ShapeDtypeStruct((1, rows), jnp.float32),
            ),
            in_specs=[anywhere, anywhere, vmem, smem, smem],
            out_specs=(vmem, vmem, vmem),
            scratch_shapes=[block] * 6
            + [total] * 2
            + [
                pltpu.SemaphoreType.DMA((2,)),
                pltpu.SemaphoreType.DMA((4, CHUNKS)),
                pltpu.SemaphoreType.DMA((4, CHUNKS)),
            ],
            compiler_params=pltpu.CompilerParams(
                collective_id=0, has_side_effects=True, vmem_limit_bytes=40 << 20
            ),
        )(image, text, caption, log_scale.reshape(1), bias.reshape(1))
        return grad_image, grad_text, row_loss.reshape(rows)

    spec = P(("dp", "group"), None)
    return jax.shard_map(
        body,
        mesh=mesh,
        in_specs=(spec, spec, spec, P(), P()),
        out_specs=(spec, spec, P(("dp", "group"))),
        check_vma=False,
    )
```

time: 201 us -> 178 us (0.89)
  the two profiles are of different devices: /device:TPU:400 before, /device:TPU:80 now
where the time goes in v1:
time: 178 us
  Pallas kernels  171 us (96%)
  local copies, waits for them, and re-layouts  4.17 us (2%)
  between operations  1.96 us (1%)
    pallas_call x1, Pallas kernels, body(): pl.pallas_call(functools.partial(kernel, groups, blocks), out_shape=(jax....  171 us
    unnamed x8, local copies, waits for them, and re-layouts  4.17 us

profile of v1, /device:TPU:80, one launch (start us, length us, event | category | flops | bytes accessed | tf_op | source)
XLA Modules:
  0.0 177.8 jit_solution(17675057503169015146)
XLA Ops:
  1.3 0.0 copy-start.2
  1.9 0.0 copy-done.2
  2.0 0.0 copy-start
  2.0 1.2 copy-done
  3.1 0.0 copy-start.1
  3.1 1.2 copy-done.1
  4.3 171.0 %shard_map.76 = (bf16[384,1152]{1,0:T(8,128)(2,1)S(1)}, bf16[384,1152]{1,0:T(8,128)(2,1)S(1)}, f32[1,384]{1,0:T(1,128)S(1)}) custom-call(bf16[384,1152]{1,0:T(8,128)(2,1)S(1)} %copy-done, bf16[384,1152]{1,0:T(8,128)(2,1)S(1)} %copy-done.1, s32[1,384]{1,0:T(1,128)S(1)} %copy-done.2, f32[1]{0:T(128)} %bitcast.2.log_scale, f32[1]{0:T(128)} %bitcast.3.bias), custom_call_target="tpu_custom_call" | custom-call | tf_op jit(solution)/shard_map/pallas_call | solution.py:153
  175.3 0.6 reduce
  175.9 0.9 copy.12
  176.8 0.9 copy.13
Async XLA Ops:
  1.3 0.7 copy-start.2
  2.0 1.2 copy-start
  3.1 1.2 copy-start.1

commit v2 on v1

v2 whole, which is shorter than its diff:
```python
import functools

import jax
import jax.numpy as jnp
from jax import lax
from jax.experimental import pallas as pl
from jax.experimental.pallas import tpu as pltpu
from jax.sharding import PartitionSpec as P

MESH = pl.DeviceIdType.MESH
CHUNKS = 4
XS, YS, ZS = 4, 8, 12
PLANE = XS * YS * 2
HOPS = ZS // 2


def dot_nt(a, b):
    return lax.dot_general(a, b, (((1,), (1,)), ((), ())), preferred_element_type=jnp.float32)


def dot_tn(a, b):
    return lax.dot_general(a, b, (((0,), (0,)), ((), ())), preferred_element_type=jnp.float32)


def halves(logits):
    small = jnp.exp(-jnp.abs(logits))
    loss = jnp.maximum(logits, 0.0) + jnp.log1p(small)
    chance = jnp.where(logits >= 0, 1.0, small) / (1.0 + small)
    return loss, chance


def kernel(
    groups, blocks,
    image, text, caption, log_scale, bias,
    grad_image, grad_text, row_loss,
    own_image, own_text, near_text, near_image, far_text, far_image,
    near_pass, far_pass, sum_image, sum_text,
    load_sem, far_send, far_recv, near_send, near_recv, pass_send, pass_recv,
):
    rows = image.shape[0]
    part = rows // CHUNKS
    me = lax.axis_index("dp") * groups + lax.axis_index("group")
    z, x, y, core = me // PLANE, lax.rem(me // (2 * YS), XS), lax.rem(me // 2, YS), lax.rem(me, 2)

    def block(at):
        at = lax.rem(at + blocks, blocks)
        return (at // groups, lax.rem(at, groups))

    def place(z, x, y, core):
        return block(((z * XS + x) * YS + y) * 2 + core)

    high = y // (YS // 2)
    edge = (XS - 1) * high
    across = 2 * high - 1
    opposite = y - across * (YS // 2)
    is_edge = x == edge
    plane_at = lax.rem(me, PLANE)
    last = plane_at == PLANE - 1
    first = plane_at == 0
    text_pass = jnp.logical_and(y == 0, core == 0)
    image_pass = jnp.logical_and(y == YS - 1, core == 1)

    near_source = place(z, edge, y, core)
    near_goal = place(z + across, XS - 1 - edge, opposite, core)

    def near_stop(q):
        return place(z, q, y, core)

    def near_sender(q):
        return place(z + across, q, opposite, core)

    text_source = place(z, XS - 1, YS - 1, 1)
    text_goal = place(z + 2, 0, 0, 0)
    image_source = place(z, 0, 0, 0)
    image_goal = place(z - 2, XS - 1, YS - 1, 1)

    def text_stop(j):
        return place(z, j, 0, 0)

    def image_stop(j):
        return place(z, j, YS - 1, 1)

    leap = PLANE + 1
    regular = [block(me + step) for step in (leap, -leap, PLANE, -PLANE, groups, -groups)]
    barrier = pltpu.get_barrier_semaphore()

    def greet(peers):
        for peer in peers:
            pl.semaphore_signal(barrier, inc=1, device_id=peer, device_id_type=MESH)

    greet(regular)

    @pl.when(is_edge)
    def _():
        for n in range(1, XS):
            greet([near_stop(edge - across * n), near_sender(XS - 1 - edge + across * n)])

    @pl.when(jnp.logical_not(is_edge))
    def _():
        greet([near_source, near_goal])

    @pl.when(last)
    def _():
        greet([text_stop(j) for j in range(XS)] + [place(z + 2, j, YS - 1, 1) for j in range(XS)])

    @pl.when(first)
    def _():
        greet([image_stop(j) for j in range(XS)] + [place(z - 2, j, 0, 0) for j in range(XS)])

    @pl.when(text_pass)
    def _():
        greet([text_source, text_goal])

    @pl.when(image_pass)
    def _():
        greet([image_source, image_goal])

    def one_if(condition):
        return condition.astype(jnp.int32)

    pl.semaphore_wait(
        barrier,
        len(regular) + 2
        + (2 * XS - 4) * one_if(is_edge)
        + 2 * XS * (one_if(last) + one_if(first))
        + 2 * (one_if(text_pass) + one_if(image_pass)),
    )

    def rows_of(k):
        return pl.ds(pl.multiple_of(k * part, part), part)

    def send(source, target, sent, got, peer):
        return pltpu.make_async_remote_copy(
            src_ref=source, dst_ref=target, send_sem=sent, recv_sem=got,
            device_id=peer, device_id_type=MESH,
        )

    inputs = (text, image)
    far_bufs = (far_text, far_image)
    near_bufs = (near_text, near_image)

    def far_first(flow, k, peer=None, source=None, sent=None):
        return send(
            inputs[flow].at[rows_of(k)] if source is None else source,
            far_bufs[flow].at[0, rows_of(k)],
            far_send.at[flow, 0, k] if sent is None else sent,
            far_recv.at[flow, 0, k],
            block(me + (leap, -leap)[flow]) if peer is None else peer,
        )

    def far_next(flow, s, k):
        return send(
            far_bufs[flow].at[s - 1, rows_of(k)], far_bufs[flow].at[s, rows_of(k)],
            far_send.at[flow, s, k], far_recv.at[flow, s, k], block(me + (PLANE, -PLANE)[flow]),
        )

    def near(flow, k, peer=None, source=None, sent=None):
        return send(
            inputs[flow].at[rows_of(k)] if source is None else source,
            near_bufs[flow].at[rows_of(k)],
            near_send.at[flow, k] if sent is None else sent,
            near_recv.at[flow, k],
            block(me + (groups, -groups)[flow]) if peer is None else peer,
        )

    def near_detour(flow, k):
        return send(
            inputs[flow].at[rows_of(k)], near_pass, near_send.at[flow, k], pass_recv.at[0], near_stop(k)
        )

    def far_detour(flow, k):
        return send(
            inputs[flow].at[rows_of(k)], far_pass, far_send.at[flow, 0, k], pass_recv.at[1],
            (text_stop, image_stop)[flow](k),
        )

    far_special = (last, first)
    near_special = (
        jnp.logical_and(is_edge, high == 1),
        jnp.logical_and(is_edge, high == 0),
    )

    for flow in (0, 1):
        @pl.when(far_special[flow])
        def _():
            if flow == 0:
                for k in range(CHUNKS):
                    far_detour(flow, k).start()
            else:
                for k in reversed(range(CHUNKS)):
                    far_detour(flow, k).start()

        @pl.when(near_special[flow])
        def _():
            for k in range(CHUNKS):
                if k == (XS - 1, 0)[flow]:
                    near(flow, k).start()
                else:
                    near_detour(flow, k).start()

    def open_far(k, _):
        for flow in (0, 1):
            @pl.when(jnp.logical_not(far_special[flow]))
            def _():
                far_first(flow, k).start()

        return 0

    def open_near(k, _):
        for flow in (0, 1):
            @pl.when(jnp.logical_not(near_special[flow]))
            def _():
                near(flow, k).start()

        return 0

    lax.fori_loop(0, CHUNKS, open_far, 0)
    lax.fori_loop(0, CHUNKS, open_near, 0)

    loads = [
        pltpu.make_async_copy(image, own_image, load_sem.at[0]),
        pltpu.make_async_copy(text, own_text, load_sem.at[1]),
    ]
    for load in loads:
        load.start()

    text_hand = far_first(0, x, text_goal, far_pass, pass_send.at[1])
    image_hand = far_first(1, x, image_goal, far_pass, pass_send.at[1])
    near_text_hand = near(0, x, near_goal, near_pass, pass_send.at[0])
    near_image_hand = near(1, x, near_goal, near_pass, pass_send.at[0])
    pass_text = jnp.logical_and(jnp.logical_not(is_edge), high == 1)
    pass_image = jnp.logical_and(jnp.logical_not(is_edge), high == 0)
    hands = (
        (text_pass, text_hand),
        (image_pass, image_hand),
        (pass_text, near_text_hand),
        (pass_image, near_image_hand),
    )

    for n, (mine, hand) in enumerate(hands):
        @pl.when(mine)
        def _():
            send(
                text.at[rows_of(0)], (far_pass, near_pass)[n // 2], pass_send.at[1 - n // 2],
                pass_recv.at[1 - n // 2], block(me + groups),
            ).wait_recv()
            hand.start()

    def forward(i, _):
        s, k = i // CHUNKS, lax.rem(i, CHUNKS)
        for flow in (0, 1):
            @pl.when(s == 1)
            def _():
                far_first(flow, k).wait_recv()

            @pl.when(s > 1)
            def _():
                far_next(flow, s - 1, k).wait_recv()

            far_next(flow, s, k).start()
        return 0

    lax.fori_loop(CHUNKS, 2 * CHUNKS, forward, 0)
    for load in loads:
        load.wait()

    scale = jnp.exp(jnp.full((1, rows), log_scale[0], jnp.float32))
    shift = bias[0]
    row_loss[...] = jnp.zeros_like(row_loss)

    def own(k, _):
        texts = own_text[rows_of(k), :]
        logits = scale * dot_nt(texts, own_image[...]) + shift
        loss, chance = halves(logits)
        line = lax.broadcasted_iota(jnp.int32, (part, rows), 0) + k * part
        positive = line == caption[...]
        loss = loss - jnp.where(positive, logits, 0.0)
        coef = (chance - positive.astype(jnp.float32)).astype(jnp.bfloat16)
        row_loss[...] += jnp.sum(loss, axis=0, keepdims=True)
        sum_text[rows_of(k), :] = jnp.dot(coef, own_image[...], preferred_element_type=jnp.float32)
        add = dot_tn(coef, texts)

        @pl.when(k == 0)
        def _():
            sum_image[...] = add

        @pl.when(k > 0)
        def _():
            sum_image[...] += add

        return 0

    lax.fori_loop(0, CHUNKS, own, 0)
    lax.fori_loop(2 * CHUNKS, HOPS * CHUNKS, forward, 0)

    def meet_text(texts):
        loss, chance = halves(scale * dot_nt(texts, own_image[...]) + shift)
        row_loss[...] += jnp.sum(loss, axis=0, keepdims=True)
        sum_image[...] += dot_tn(chance.astype(jnp.bfloat16), texts)

    def meet_image(images):
        _, chance = halves(scale * dot_nt(images, own_text[...]) + shift)
        sum_text[...] += dot_tn(chance.astype(jnp.bfloat16), images)

    def near_pair(k, _):
        near(0, k).wait_recv()
        meet_text(near_text[rows_of(k), :])
        near(1, k).wait_recv()
        meet_image(near_image[rows_of(k), :])
        return 0

    def far_pair(k, _):
        far_next(0, HOPS - 1, k).wait_recv()
        meet_text(far_text[HOPS - 1, rows_of(k), :])
        far_next(1, HOPS - 1, k).wait_recv()
        meet_image(far_image[HOPS - 1, rows_of(k), :])
        return 0

    lax.fori_loop(0, CHUNKS, near_pair, 0)
    lax.fori_loop(0, CHUNKS, far_pair, 0)
    wide = jnp.exp(jnp.full((1, image.shape[1]), log_scale[0], jnp.float32))
    grad_image[...] = (wide * sum_image[...]).astype(grad_image.dtype)
    grad_text[...] = (wide * sum_text[...]).astype(grad_text.dtype)
    row_loss[...] = row_loss[...] / jnp.float32(3 * rows)

    def drain(k, _):
        for flow in (0, 1):
            far_first(flow, k).wait_send()
            near(flow, k).wait_send()
        return 0

    def drain_next(i, _):
        for flow in (0, 1):
            far_next(flow, i // CHUNKS, lax.rem(i, CHUNKS)).wait_send()
        return 0

    lax.fori_loop(0, CHUNKS, drain, 0)
    lax.fori_loop(CHUNKS, HOPS * CHUNKS, drain_next, 0)
    for mine, hand in hands:
        @pl.when(mine)
        def _():
            hand.wait_send()


def solution(mesh):
    groups = mesh.shape["group"]
    blocks = mesh.shape["dp"] * groups

    def body(image, text, caption, log_scale, bias):
        rows, width = image.shape
        block = pltpu.VMEM((rows, width), jnp.bfloat16)
        relayed = pltpu.VMEM((HOPS, rows, width), jnp.bfloat16)
        piece = pltpu.VMEM((rows // CHUNKS, width), jnp.bfloat16)
        total = pltpu.VMEM((rows, width), jnp.float32)
        vmem = pl.BlockSpec(memory_space=pltpu.VMEM)
        smem = pl.BlockSpec(memory_space=pltpu.SMEM)
        anywhere = pl.BlockSpec(memory_space=pl.ANY)
        grad_image, grad_text, row_loss = pl.pallas_call(
            functools.partial(kernel, groups, blocks),
            out_shape=(
                jax.ShapeDtypeStruct((rows, width), jnp.bfloat16),
                jax.ShapeDtypeStruct((rows, width), jnp.bfloat16),
                jax.ShapeDtypeStruct((1, rows), jnp.float32),
            ),
            in_specs=[anywhere, anywhere, vmem, smem, smem],
            out_specs=(vmem, vmem, vmem),
            scratch_shapes=[block] * 4
            + [relayed] * 2
            + [piece] * 2
            + [total] * 2
            + [
                pltpu.SemaphoreType.DMA((2,)),
                pltpu.SemaphoreType.DMA((2, HOPS, CHUNKS)),
                pltpu.SemaphoreType.DMA((2, HOPS, CHUNKS)),
                pltpu.SemaphoreType.DMA((2, CHUNKS)),
                pltpu.SemaphoreType.DMA((2, CHUNKS)),
                pltpu.SemaphoreType.DMA((2,)),
                pltpu.SemaphoreType.DMA((2,)),
            ],
            compiler_params=pltpu.CompilerParams(
                collective_id=0, has_side_effects=True, vmem_limit_bytes=58 << 20
            ),
        )(image, text, caption, log_scale.reshape(1), bias.reshape(1))
        return grad_image, grad_text, row_loss.reshape(rows)

    spec = P(("dp", "group"), None)
    return jax.shard_map(
        body,
        mesh=mesh,
        in_specs=(spec, spec, spec, P(), P()),
        out_specs=(spec, spec, P(("dp", "group"))),
        check_vma=False,
    )
```

time: 178 us -> 156 us (0.88)
  the two profiles are of different devices: /device:TPU:80 before, /device:TPU:4 now
where the time goes in v2:
time: 156 us
  Pallas kernels  150 us (96%)
  local copies, waits for them, and re-layouts  3.77 us (2%)
  between operations  1.94 us (1%)
    pallas_call x1, Pallas kernels, body(): pl.pallas_call(functools.partial(kernel, groups, blocks), out_shape=(jax....  150 us
    unnamed x6, local copies, waits for them, and re-layouts  3.77 us

profile of v2, /device:TPU:4, one launch (start us, length us, event | category | flops | bytes accessed | tf_op | source)
XLA Modules:
  0.0 156.1 jit_solution(10250295630436811651)
XLA Ops:
  1.9 149.8 %shard_map.76 = (bf16[384,1152]{1,0:T(8,128)(2,1)}, bf16[384,1152]{1,0:T(8,128)(2,1)}, f32[1,384]{1,0:T(1,128)}) custom-call(bf16[384,1152]{1,0:T(8,128)(2,1)} %image.1, bf16[384,1152]{1,0:T(8,128)(2,1)} %text.1, s32[1,384]{1,0:T(1,128)} %caption.1, f32[1]{0:T(128)} %bitcast.2.log_scale, f32[1]{0:T(128)} %bitcast.3.bias), custom_call_target="tpu_custom_call" | custom-call | tf_op jit(solution)/shard_map/pallas_call | solution.py:358
  151.7 0.0 copy-start.1
  151.7 0.6 copy-done.1
  152.3 0.6 reduce
  152.9 0.0 copy-start
  152.9 2.2 %copy.12 = bf16[384,1152]{1,0:T(8,128)(2,1)} copy(bf16[384,1152]{1,0:T(8,128)(2,1)} %get-tuple-element.12) | data formatting | bytes 1769472
  155.2 0.0 copy-done
  155.2 0.9 copy.13
Async XLA Ops:
  151.7 0.6 copy-start.1
  152.9 2.2 %copy-start = (bf16[384,1152]{1,0:T(8,128)(2,1)S(1)}, bf16[384,1152]{1,0:T(8,128)(2,1)}, u32[]{:S(2)}) copy-start(bf16[384,1152]{1,0:T(8,128)(2,1)} %get-tuple-element.13) | copy-start | bytes 2654212

commit v3 on v2

--- a/solution.py
+++ b/solution.py
@@ -81,50 +81,119 @@
         return place(z, j, YS - 1, 1)
 
     leap = PLANE + 1
-    regular = [block(me + step) for step in (leap, -leap, PLANE, -PLANE, groups, -groups)]
     barrier = pltpu.get_barrier_semaphore()
 
-    def greet(peers):
+    def one_if(condition):
+        return condition.astype(jnp.int32)
+
+    def tell(peers):
         for peer in peers:
             pl.semaphore_signal(barrier, inc=1, device_id=peer, device_id_type=MESH)
 
-    greet(regular)
+    top = z == ZS - 1
+    goal_edge = jnp.logical_and(is_edge, high == 1)
+    senders = [(step, block(me - step)) for step in (PLANE, groups)]
+    others = [(step, block(me + step)) for step in (PLANE, groups)]
+
+    for step, peer in senders:
+        @pl.when(me >= step)
+        def _():
+            tell([peer])
+
+    @pl.when(jnp.logical_and(jnp.logical_not(first), me >= leap))
+    def _():
+        tell([block(me - leap)])
+
+    for step, peer in others:
+        @pl.when(me + step < blocks)
+        def _():
+            tell([peer])
+
+    @pl.when(jnp.logical_and(jnp.logical_not(last), me + leap < blocks))
+    def _():
+        tell([block(me + leap)])
 
     @pl.when(is_edge)
     def _():
         for n in range(1, XS):
-            greet([near_stop(edge - across * n), near_sender(XS - 1 - edge + across * n)])
+            @pl.when(jnp.logical_not(jnp.logical_and(top, high == 1)))
+            def _():
+                tell([near_sender(XS - 1 - edge + across * n)])
+
+    low_pass = jnp.logical_and(jnp.logical_not(is_edge), high == 0)
 
     @pl.when(jnp.logical_not(is_edge))
     def _():
-        greet([near_source, near_goal])
-
-    @pl.when(last)
-    def _():
-        greet([text_stop(j) for j in range(XS)] + [place(z + 2, j, YS - 1, 1) for j in range(XS)])
+        tell([near_source])
+
+    image_senders = [place(z + 2, j, YS - 1, 1) for j in range(XS)]
+
+    @pl.when(jnp.logical_and(last, z < ZS - 2))
+    def _():
+        tell(image_senders)
 
     @pl.when(first)
     def _():
-        greet([image_stop(j) for j in range(XS)] + [place(z - 2, j, 0, 0) for j in range(XS)])
+        tell([place(z - 2, j, 0, 0) for j in range(XS)])
 
     @pl.when(text_pass)
     def _():
-        greet([text_source, text_goal])
+        tell([text_source])
 
     @pl.when(image_pass)
     def _():
-        greet([image_source, image_goal])
-
-    def one_if(condition):
-        return condition.astype(jnp.int32)
-
+        tell([image_source])
+
+    late_count = (
+        one_if(z == 0) * (1 + one_if(jnp.logical_not(first)))
+        + one_if(me < groups)
+        + one_if(jnp.logical_and(low_pass, z == 0))
+        + one_if(jnp.logical_and(image_pass, z < 2))
+    )
     pl.semaphore_wait(
         barrier,
-        len(regular) + 2
-        + (2 * XS - 4) * one_if(is_edge)
-        + 2 * XS * (one_if(last) + one_if(first))
-        + 2 * (one_if(text_pass) + one_if(image_pass)),
+        6 - one_if(first) - one_if(last)
+        + (XS - 1) * one_if(is_edge) + one_if(jnp.logical_not(is_edge))
+        + XS * (one_if(last) + one_if(first))
+        + one_if(text_pass) + one_if(image_pass)
+        + (XS - 1) * one_if(jnp.logical_and(goal_edge, top))
+        + XS * one_if(jnp.logical_and(last, z >= ZS - 2))
+        - late_count,
     )
+
+    for step, peer in senders:
+        @pl.when(me < step)
+        def _():
+            tell([peer])
+
+    @pl.when(jnp.logical_and(jnp.logical_not(first), me < leap))
+    def _():
+        tell([block(me - leap)])
+
+    @pl.when(jnp.logical_and(low_pass, z == 0))
+    def _():
+        tell([near_goal])
+
+    @pl.when(jnp.logical_and(image_pass, z < 2))
+    def _():
+        tell([image_goal])
+
+    for step, peer in others:
+        @pl.when(me + step >= blocks)
+        def _():
+            tell([peer])
+
+    @pl.when(jnp.logical_and(jnp.logical_not(last), me + leap >= blocks))
+    def _():
+        tell([block(me + leap)])
+
+    @pl.when(jnp.logical_and(goal_edge, top))
+    def _():
+        tell([near_sender(n) for n in range(1, XS)])
+
+    @pl.when(jnp.logical_and(last, z >= ZS - 2))
+    def _():
+        tell(image_senders)
 
     def rows_of(k):
         return pl.ds(pl.multiple_of(k * part, part), part)
@@ -180,15 +249,11 @@
         jnp.logical_and(is_edge, high == 0),
     )
 
-    for flow in (0, 1):
+    def open_special(flow):
         @pl.when(far_special[flow])
         def _():
-            if flow == 0:
-                for k in range(CHUNKS):
-                    far_detour(flow, k).start()
-            else:
-                for k in reversed(range(CHUNKS)):
-                    far_detour(flow, k).start()
+            for k in range(CHUNKS):
+                far_detour(flow, k if flow == 0 else CHUNKS - 1 - k).start()
 
         @pl.when(near_special[flow])
         def _():
@@ -198,24 +263,43 @@
                 else:
                     near_detour(flow, k).start()
 
-    def open_far(k, _):
-        for flow in (0, 1):
-            @pl.when(jnp.logical_not(far_special[flow]))
-            def _():
-                far_first(flow, k).start()
-
-        return 0
-
-    def open_near(k, _):
-        for flow in (0, 1):
-            @pl.when(jnp.logical_not(near_special[flow]))
-            def _():
-                near(flow, k).start()
-
-        return 0
-
-    lax.fori_loop(0, CHUNKS, open_far, 0)
-    lax.fori_loop(0, CHUNKS, open_near, 0)
+    def open_flows(flows):
+        def open_far(k, _):
+            for flow in flows:
+                @pl.when(jnp.logical_not(far_special[flow]))
+                def _():
+                    far_first(flow, k).start()
+
+            return 0
+
+        def open_near(k, _):
+            for flow in flows:
+                @pl.when(jnp.logical_not(near_special[flow]))
+                def _():
+                    near(flow, k).start()
+
+            return 0
+
+        for flow in flows:
+            open_special(flow)
+        lax.fori_loop(0, CHUNKS, open_far, 0)
+        lax.fori_loop(0, CHUNKS, open_near, 0)
+
+    @pl.when(z > 0)
+    def _():
+        open_flows((0, 1))
+
+    @pl.when(z == 0)
+    def _():
+        open_flows((0,))
+
+    @pl.when(late_count > 0)
+    def _():
+        pl.semaphore_wait(barrier, late_count)
+
+    @pl.when(z == 0)
+    def _():
+        open_flows((1,))
 
     loads = [
         pltpu.make_async_copy(image, own_image, load_sem.at[0]),
@@ -378,7 +462,7 @@
                 pltpu.SemaphoreType.DMA((2,)),
             ],
             compiler_params=pltpu.CompilerParams(
-                collective_id=0, has_side_effects=True, vmem_limit_bytes=58 << 20
+                collective_id=0, has_side_effects=True, vmem_limit_bytes=54_250_000
             ),
         )(image, text, caption, log_scale.reshape(1), bias.reshape(1))
         return grad_image, grad_text, row_loss.reshape(rows)

time: 156 us -> 153 us (0.981)
  local copies, waits for them, and re-layouts: 3.77 us -> 1.84 us
    unnamed x6 -> x4, local copies, waits for them, and re-layouts: 3.77 us -> 1.84 us
where the time goes in v3:
time: 153 us
  Pallas kernels  149 us (97%)
  between operations  1.95 us (1%)
  local copies, waits for them, and re-layouts  1.84 us (1%)
    pallas_call x1, Pallas kernels, body(): pl.pallas_call(functools.partial(kernel, groups, blocks), out_shape=(jax....  149 us

profile of v3, /device:TPU:4, one launch (start us, length us, event | category | flops | bytes accessed | tf_op | source)
XLA Modules:
  0.0 153.1 jit_solution(1294093738009600391)
XLA Ops:
  1.3 0.0 copy-start
  1.9 0.0 copy-done
  2.0 148.7 %shard_map.76 = (bf16[384,1152]{1,0:T(8,128)(2,1)S(1)}, bf16[384,1152]{1,0:T(8,128)(2,1)S(1)}, f32[1,384]{1,0:T(1,128)S(1)}) custom-call(bf16[384,1152]{1,0:T(8,128)(2,1)} %image.1, bf16[384,1152]{1,0:T(8,128)(2,1)} %text.1, s32[1,384]{1,0:T(1,128)S(1)} %copy-done, f32[1]{0:T(128)} %bitcast.2.log_scale, f32[1]{0:T(128)} %bitcast.3.bias), custom_call_target="tpu_custom_call" | custom-call | tf_op jit(solution)/shard_map/pallas_call | solution.py:442
  150.7 0.6 reduce
  151.3 0.9 copy.12
  152.2 0.9 copy.13
Async XLA Ops:
  1.3 0.7 copy-start

commit v4 on v3

--- a/solution.py
+++ b/solution.py
@@ -12,6 +12,7 @@
 XS, YS, ZS = 4, 8, 12
 PLANE = XS * YS * 2
 HOPS = ZS // 2
+TURNED = 1
 
 
 def dot_nt(a, b):
@@ -32,10 +33,10 @@
 def kernel(
     groups, blocks,
     image, text, caption, log_scale, bias,
-    grad_image, grad_text, row_loss,
+    grad_image, grad_text, loss_out,
     own_image, own_text, near_text, near_image, far_text, far_image,
-    near_pass, far_pass, sum_image, sum_text,
-    load_sem, far_send, far_recv, near_send, near_recv, pass_send, pass_recv,
+    near_pass, far_pass, turned, sum_image, sum_text, row_loss,
+    load_sem, far_send, far_recv, near_send, near_recv, pass_send, pass_recv, turned_sem,
 ):
     rows = image.shape[0]
     part = rows // CHUNKS
@@ -143,6 +144,31 @@
     @pl.when(image_pass)
     def _():
         tell([image_source])
+
+    low_mid = z == HOPS - 1
+    high_mid = z == HOPS
+    text_turn = jnp.logical_and(high_mid, jnp.logical_not(last))
+    image_turn = jnp.logical_and(low_mid, jnp.logical_not(first))
+    text_turn_pass = jnp.logical_and(jnp.logical_and(text_pass, low_mid), x == TURNED)
+    image_turn_pass = jnp.logical_and(jnp.logical_and(image_pass, high_mid), x == TURNED)
+    text_turn_to = block(me - PLANE + 1)
+    image_turn_to = block(me + PLANE - 1)
+
+    @pl.when(text_turn)
+    def _():
+        tell([text_turn_to])
+
+    @pl.when(image_turn)
+    def _():
+        tell([image_turn_to])
+
+    @pl.when(jnp.logical_and(first, low_mid))
+    def _():
+        tell([text_stop(TURNED)])
+
+    @pl.when(jnp.logical_and(last, high_mid))
+    def _():
+        tell([image_stop(TURNED)])
 
     late_count = (
         one_if(z == 0) * (1 + one_if(jnp.logical_not(first)))
@@ -158,6 +184,8 @@
         + one_if(text_pass) + one_if(image_pass)
         + (XS - 1) * one_if(jnp.logical_and(goal_edge, top))
         + XS * one_if(jnp.logical_and(last, z >= ZS - 2))
+        + one_if(text_turn) + one_if(image_turn)
+        + one_if(text_turn_pass) + one_if(image_turn_pass)
         - late_count,
     )
 
@@ -266,24 +294,24 @@
     def open_flows(flows):
         def open_far(k, _):
             for flow in flows:
-                @pl.when(jnp.logical_not(far_special[flow]))
+                turns = jnp.logical_and((text_turn, image_turn)[flow], k == TURNED)
+
+                @pl.when(jnp.logical_not(jnp.logical_or(far_special[flow], turns)))
                 def _():
                     far_first(flow, k).start()
 
-            return 0
-
-        def open_near(k, _):
-            for flow in flows:
-                @pl.when(jnp.logical_not(near_special[flow]))
+                @pl.when(turns)
                 def _():
-                    near(flow, k).start()
+                    send(
+                        inputs[flow].at[rows_of(k)], turned, far_send.at[flow, 0, k],
+                        turned_sem.at[1], (text_turn_to, image_turn_to)[flow],
+                    ).start()
 
             return 0
 
         for flow in flows:
             open_special(flow)
         lax.fori_loop(0, CHUNKS, open_far, 0)
-        lax.fori_loop(0, CHUNKS, open_near, 0)
 
     @pl.when(z > 0)
     def _():
@@ -308,43 +336,84 @@
     for load in loads:
         load.start()
 
-    text_hand = far_first(0, x, text_goal, far_pass, pass_send.at[1])
-    image_hand = far_first(1, x, image_goal, far_pass, pass_send.at[1])
-    near_text_hand = near(0, x, near_goal, near_pass, pass_send.at[0])
-    near_image_hand = near(1, x, near_goal, near_pass, pass_send.at[0])
     pass_text = jnp.logical_and(jnp.logical_not(is_edge), high == 1)
-    pass_image = jnp.logical_and(jnp.logical_not(is_edge), high == 0)
     hands = (
-        (text_pass, text_hand),
-        (image_pass, image_hand),
-        (pass_text, near_text_hand),
-        (pass_image, near_image_hand),
+        (jnp.logical_and(text_pass, jnp.logical_not(text_turn_pass)),
+         far_first(0, x, text_goal, far_pass, pass_send.at[1])),
+        (jnp.logical_and(image_pass, jnp.logical_not(image_turn_pass)),
+         far_first(1, x, image_goal, far_pass, pass_send.at[1])),
+        (text_turn_pass,
+         send(far_pass, turned, pass_send.at[1], turned_sem.at[1], place(z, 0, 0, 0))),
+        (image_turn_pass,
+         send(far_pass, turned, pass_send.at[1], turned_sem.at[1], place(z, XS - 1, YS - 1, 1))),
+        (pass_text, near(0, x, near_goal, near_pass, pass_send.at[0])),
+        (low_pass, near(1, x, near_goal, near_pass, pass_send.at[0])),
     )
 
     for n, (mine, hand) in enumerate(hands):
         @pl.when(mine)
         def _():
             send(
-                text.at[rows_of(0)], (far_pass, near_pass)[n // 2], pass_send.at[1 - n // 2],
-                pass_recv.at[1 - n // 2], block(me + groups),
+                text.at[rows_of(0)], (far_pass, near_pass)[n // 4], pass_send.at[1 - n // 4],
+                pass_recv.at[1 - n // 4], block(me + groups),
             ).wait_recv()
             hand.start()
+
+    turn_step = one_if(z < HOPS) * (HOPS - z) + one_if(z >= HOPS) * (z - HOPS + 1)
+    turn_cases = (
+        (jnp.logical_and(z > 1, z < HOPS), send(
+            turned, turned, turned_sem.at[0], turned_sem.at[1], block(me - PLANE))),
+        (z == 1, send(
+            turned, far_text.at[HOPS - 1, rows_of(TURNED)], turned_sem.at[0],
+            far_recv.at[0, HOPS - 1, TURNED], block(me - PLANE))),
+        (jnp.logical_and(z >= HOPS, z < ZS - 2), send(
+            turned, turned, turned_sem.at[0], turned_sem.at[1], block(me + PLANE))),
+        (z == ZS - 2, send(
+            turned, far_image.at[HOPS - 1, rows_of(TURNED)], turned_sem.at[0],
+            far_recv.at[1, HOPS - 1, TURNED], block(me + PLANE))),
+    )
+
+    def moved(flow, s, k):
+        gone = s == ((z - HOPS), (HOPS - 1 - z))[flow]
+        return jnp.logical_and(gone, k == TURNED)
 
     def forward(i, _):
         s, k = i // CHUNKS, lax.rem(i, CHUNKS)
         for flow in (0, 1):
-            @pl.when(s == 1)
+            stays = jnp.logical_not(moved(flow, s, k))
+
+            @pl.when(jnp.logical_and(stays, s == 1))
             def _():
                 far_first(flow, k).wait_recv()
 
-            @pl.when(s > 1)
+            @pl.when(jnp.logical_and(stays, s > 1))
             def _():
                 far_next(flow, s - 1, k).wait_recv()
 
-            far_next(flow, s, k).start()
+            @pl.when(stays)
+            def _():
+                far_next(flow, s, k).start()
+
+        for mine, hand in turn_cases:
+            @pl.when(jnp.logical_and(mine, jnp.logical_and(s == turn_step, k == TURNED)))
+            def _():
+                send(
+                    text.at[rows_of(0)], turned, turned_sem.at[0], turned_sem.at[1], block(me + groups)
+                ).wait_recv()
+                hand.start()
+
+        return 0
+
+    def open_near(k, _):
+        for flow in (0, 1):
+            @pl.when(jnp.logical_not(near_special[flow]))
+            def _():
+                near(flow, k).start()
+
         return 0
 
     lax.fori_loop(CHUNKS, 2 * CHUNKS, forward, 0)
+    lax.fori_loop(0, CHUNKS, open_near, 0)
     for load in loads:
         load.wait()
 
@@ -405,7 +474,7 @@
     wide = jnp.exp(jnp.full((1, image.shape[1]), log_scale[0], jnp.float32))
     grad_image[...] = (wide * sum_image[...]).astype(grad_image.dtype)
     grad_text[...] = (wide * sum_text[...]).astype(grad_text.dtype)
-    row_loss[...] = row_loss[...] / jnp.float32(3 * rows)
+    loss_out[...] = (row_loss[...] / jnp.float32(3 * rows)).reshape(rows)
 
     def drain(k, _):
         for flow in (0, 1):
@@ -414,13 +483,17 @@
         return 0
 
     def drain_next(i, _):
+        s, k = i // CHUNKS, lax.rem(i, CHUNKS)
         for flow in (0, 1):
-            far_next(flow, i // CHUNKS, lax.rem(i, CHUNKS)).wait_send()
+            @pl.when(jnp.logical_not(moved(flow, s, k)))
+            def _():
+                far_next(flow, s, k).wait_send()
+
         return 0
 
     lax.fori_loop(0, CHUNKS, drain, 0)
     lax.fori_loop(CHUNKS, HOPS * CHUNKS, drain_next, 0)
-    for mine, hand in hands:
+    for mine, hand in hands + turn_cases:
         @pl.when(mine)
         def _():
             hand.wait_send()
@@ -444,15 +517,16 @@
             out_shape=(
                 jax.ShapeDtypeStruct((rows, width), jnp.bfloat16),
                 jax.ShapeDtypeStruct((rows, width), jnp.bfloat16),
-                jax.ShapeDtypeStruct((1, rows), jnp.float32),
+                jax.ShapeDtypeStruct((rows,), jnp.float32),
             ),
             in_specs=[anywhere, anywhere, vmem, smem, smem],
             out_specs=(vmem, vmem, vmem),
             scratch_shapes=[block] * 4
             + [relayed] * 2
-            + [piece] * 2
+            + [piece] * 3
             + [total] * 2
             + [
+                pltpu.VMEM((1, rows), jnp.float32),
                 pltpu.SemaphoreType.DMA((2,)),
                 pltpu.SemaphoreType.DMA((2, HOPS, CHUNKS)),
                 pltpu.SemaphoreType.DMA((2, HOPS, CHUNKS)),
@@ -460,12 +534,13 @@
                 pltpu.SemaphoreType.DMA((2, CHUNKS)),
                 pltpu.SemaphoreType.DMA((2,)),
                 pltpu.SemaphoreType.DMA((2,)),
+                pltpu.SemaphoreType.DMA((2,)),
             ],
             compiler_params=pltpu.CompilerParams(
                 collective_id=0, has_side_effects=True, vmem_limit_bytes=54_250_000
             ),
         )(image, text, caption, log_scale.reshape(1), bias.reshape(1))
-        return grad_image, grad_text, row_loss.reshape(rows)
+        return grad_image, grad_text, row_loss
 
     spec = P(("dp", "group"), None)
     return jax.shard_map(

time: 153 us -> 147 us (0.961)
  the two profiles are of different devices: /device:TPU:4 before, /device:TPU:2 now
where the time goes in v4:
time: 147 us
  Pallas kernels  142 us (97%)
  local copies, waits for them, and re-layouts  2.42 us (2%)
  between operations  1.95 us (1%)
    pallas_call x1, Pallas kernels, body(): pl.pallas_call(functools.partial(kernel, groups, blocks), out_shape=(jax....  142 us

profile of v4, /device:TPU:2, one launch (start us, length us, event | category | flops | bytes accessed | tf_op | source)
XLA Modules:
  0.0 146.6 jit_solution(9407719238370122493)
XLA Ops:
  1.3 0.0 copy-start
  1.9 0.0 copy-done
  2.0 142.2 %shard_map.76 = (bf16[384,1152]{1,0:T(8,128)(2,1)S(1)}, bf16[384,1152]{1,0:T(8,128)(2,1)S(1)}, f32[384]{0:T(512)S(1)}) custom-call(bf16[384,1152]{1,0:T(8,128)(2,1)} %image.1, bf16[384,1152]{1,0:T(8,128)(2,1)} %text.1, s32[1,384]{1,0:T(1,128)S(1)} %copy-done, f32[1]{0:T(128)} %bitcast.2.log_scale, f32[1]{0:T(128)} %bitcast.3.bias), custom_call_target="tpu_custom_call" | custom-call | tf_op jit(solution)/shard_map/pallas_call | solution.py:515
  144.2 0.9 copy.13
  145.1 0.9 copy.14
  146.0 0.6 copy.15
Async XLA Ops:
  1.3 0.7 copy-start

commit v5 on v4

--- a/solution.py
+++ b/solution.py
@@ -32,10 +32,10 @@
 
 def kernel(
     groups, blocks,
-    image, text, caption, log_scale, bias,
+    image, text, caption_in, log_scale, bias,
     grad_image, grad_text, loss_out,
     own_image, own_text, near_text, near_image, far_text, far_image,
-    near_pass, far_pass, turned, sum_image, sum_text, row_loss,
+    near_pass, far_pass, turned, sum_image, sum_text, row_loss, caption,
     load_sem, far_send, far_recv, near_send, near_recv, pass_send, pass_recv, turned_sem,
 ):
     rows = image.shape[0]
@@ -283,14 +283,6 @@
             for k in range(CHUNKS):
                 far_detour(flow, k if flow == 0 else CHUNKS - 1 - k).start()
 
-        @pl.when(near_special[flow])
-        def _():
-            for k in range(CHUNKS):
-                if k == (XS - 1, 0)[flow]:
-                    near(flow, k).start()
-                else:
-                    near_detour(flow, k).start()
-
     def open_flows(flows):
         def open_far(k, _):
             for flow in flows:
@@ -332,6 +324,7 @@
     loads = [
         pltpu.make_async_copy(image, own_image, load_sem.at[0]),
         pltpu.make_async_copy(text, own_text, load_sem.at[1]),
+        pltpu.make_async_copy(caption_in, caption, load_sem.at[2]),
     ]
     for load in loads:
         load.start()
@@ -350,14 +343,19 @@
         (low_pass, near(1, x, near_goal, near_pass, pass_send.at[0])),
     )
 
-    for n, (mine, hand) in enumerate(hands):
-        @pl.when(mine)
-        def _():
-            send(
-                text.at[rows_of(0)], (far_pass, near_pass)[n // 4], pass_send.at[1 - n // 4],
-                pass_recv.at[1 - n // 4], block(me + groups),
-            ).wait_recv()
-            hand.start()
+    def hand_on(range_of):
+        for n in range_of:
+            mine, hand = hands[n]
+
+            @pl.when(mine)
+            def _():
+                send(
+                    text.at[rows_of(0)], (far_pass, near_pass)[n // 4], pass_send.at[1 - n // 4],
+                    pass_recv.at[1 - n // 4], block(me + groups),
+                ).wait_recv()
+                hand.start()
+
+    hand_on(range(4))
 
     turn_step = one_if(z < HOPS) * (HOPS - z) + one_if(z >= HOPS) * (z - HOPS + 1)
     turn_cases = (
@@ -413,6 +411,15 @@
         return 0
 
     lax.fori_loop(CHUNKS, 2 * CHUNKS, forward, 0)
+    for flow in (0, 1):
+        @pl.when(near_special[flow])
+        def _():
+            for k in range(CHUNKS):
+                if k == (XS - 1, 0)[flow]:
+                    near(flow, k).start()
+                else:
+                    near_detour(flow, k).start()
+
     lax.fori_loop(0, CHUNKS, open_near, 0)
     for load in loads:
         load.wait()
@@ -443,8 +450,13 @@
 
         return 0
 
-    lax.fori_loop(0, CHUNKS, own, 0)
-    lax.fori_loop(2 * CHUNKS, HOPS * CHUNKS, forward, 0)
+    def own_between(k, _):
+        forward(2 * CHUNKS + k, 0)
+        return own(k, 0)
+
+    lax.fori_loop(0, CHUNKS, own_between, 0)
+    hand_on(range(4, len(hands)))
+    lax.fori_loop(3 * CHUNKS, HOPS * CHUNKS, forward, 0)
 
     def meet_text(texts):
         loss, chance = halves(scale * dot_nt(texts, own_image[...]) + shift)
@@ -497,6 +509,17 @@
         @pl.when(mine)
         def _():
             hand.wait_send()
+
+
+def store(*refs):
+    count = len(refs) // 2
+    copies = [
+        pltpu.make_async_copy(refs[n], refs[count + n], refs[-1].at[n]) for n in range(count)
+    ]
+    for copy in copies:
+        copy.start()
+    for copy in copies:
+        copy.wait()
 
 
 def solution(mesh):
@@ -519,7 +542,7 @@
                 jax.ShapeDtypeStruct((rows, width), jnp.bfloat16),
                 jax.ShapeDtypeStruct((rows,), jnp.float32),
             ),
-            in_specs=[anywhere, anywhere, vmem, smem, smem],
+            in_specs=[anywhere, anywhere, anywhere, smem, smem],
             out_specs=(vmem, vmem, vmem),
             scratch_shapes=[block] * 4
             + [relayed] * 2
@@ -527,7 +550,8 @@
             + [total] * 2
             + [
                 pltpu.VMEM((1, rows), jnp.float32),
-                pltpu.SemaphoreType.DMA((2,)),
+                pltpu.VMEM((1, rows), jnp.int32),
+                pltpu.SemaphoreType.DMA((3,)),
                 pltpu.SemaphoreType.DMA((2, HOPS, CHUNKS)),
                 pltpu.SemaphoreType.DMA((2, HOPS, CHUNKS)),
                 pltpu.SemaphoreType.DMA((2, CHUNKS)),
@@ -540,7 +564,18 @@
                 collective_id=0, has_side_effects=True, vmem_limit_bytes=54_250_000
             ),
         )(image, text, caption, log_scale.reshape(1), bias.reshape(1))
-        return grad_image, grad_text, row_loss
+        return pl.pallas_call(
+            store,
+            out_shape=(
+                jax.ShapeDtypeStruct((rows, width), jnp.bfloat16),
+                jax.ShapeDtypeStruct((rows, width), jnp.bfloat16),
+                jax.ShapeDtypeStruct((rows,), jnp.float32),
+            ),
+            in_specs=[vmem] * 3,
+            out_specs=(anywhere, anywhere, anywhere),
+            scratch_shapes=[pltpu.SemaphoreType.DMA((3,))],
+            compiler_params=pltpu.CompilerParams(vmem_limit_bytes=16 << 20),
+        )(grad_image, grad_text, row_loss)
 
     spec = P(("dp", "group"), None)
     return jax.shard_map(

time: 147 us -> 146 us (level)
  local copies, waits for them, and re-layouts: 2.42 us -> 0.02 us
    unnamed x5 -> x2, local copies, waits for them, and re-layouts: 2.42 us -> 0.02 us
where the time goes in v5:
time: 146 us; the launch traced here: 145 us
  Pallas kernels  143 us (98%)
  between operations  1.95 us (1%)
    pallas_call x1, Pallas kernels, body(): pl.pallas_call(functools.partial(kernel, groups, blocks), out_shape=(jax....  142 us

profile of v5, /device:TPU:2, one launch (start us, length us, event | category | flops | bytes accessed | tf_op | source)
XLA Modules:
  0.0 145.5 jit_solution(7096551180531181353)
XLA Ops:
  1.3 0.0 copy-start
  1.9 0.0 copy-done
  2.0 142.3 %shard_map.76 = (bf16[384,1152]{1,0:T(8,128)(2,1)S(1)}, bf16[384,1152]{1,0:T(8,128)(2,1)S(1)}, f32[384]{0:T(512)S(1)}) custom-call(bf16[384,1152]{1,0:T(8,128)(2,1)} %image.1, bf16[384,1152]{1,0:T(8,128)(2,1)} %text.1, s32[1,384]{1,0:T(1,128)S(1)} %copy-done, f32[1]{0:T(128)} %bitcast.2.log_scale, f32[1]{0:T(128)} %bitcast.3.bias), custom_call_target="tpu_custom_call" | custom-call | tf_op jit(solution)/shard_map/pallas_call | solution.py:538
  144.2 1.2 shard_map.77
Async XLA Ops:
  1.3 0.7 copy-start

commit v6 on v5

--- a/solution.py
+++ b/solution.py
@@ -482,29 +482,30 @@
         return 0
 
     lax.fori_loop(0, CHUNKS, near_pair, 0)
+    def drain(k, _):
+        for flow in (0, 1):
+            far_first(flow, k).wait_send()
+            near(flow, k).wait_send()
+        return 0
+
+    def drain_next(i, _):
+        s, k = i // CHUNKS, lax.rem(i, CHUNKS)
+        for flow in (0, 1):
+            @pl.when(jnp.logical_not(moved(flow, s, k)))
+            def _():
+                far_next(flow, s, k).wait_send()
+
+        return 0
+
+    lax.fori_loop(0, CHUNKS, drain, 0)
+    lax.fori_loop(CHUNKS, (HOPS - 1) * CHUNKS, drain_next, 0)
     lax.fori_loop(0, CHUNKS, far_pair, 0)
     wide = jnp.exp(jnp.full((1, image.shape[1]), log_scale[0], jnp.float32))
     grad_image[...] = (wide * sum_image[...]).astype(grad_image.dtype)
     grad_text[...] = (wide * sum_text[...]).astype(grad_text.dtype)
     loss_out[...] = (row_loss[...] / jnp.float32(3 * rows)).reshape(rows)
 
-    def drain(k, _):
-        for flow in (0, 1):
-            far_first(flow, k).wait_send()
-            near(flow, k).wait_send()
-        return 0
-
-    def drain_next(i, _):
-        s, k = i // CHUNKS, lax.rem(i, CHUNKS)
-        for flow in (0, 1):
-            @pl.when(jnp.logical_not(moved(flow, s, k)))
-            def _():
-                far_next(flow, s, k).wait_send()
-
-        return 0
-
-    lax.fori_loop(0, CHUNKS, drain, 0)
-    lax.fori_loop(CHUNKS, HOPS * CHUNKS, drain_next, 0)
+    lax.fori_loop((HOPS - 1) * CHUNKS, HOPS * CHUNKS, drain_next, 0)
     for mine, hand in hands + turn_cases:
         @pl.when(mine)
         def _():

time: 146 us -> 146 us (level)
  no operation moved by 1% of the time
where the time goes in v6:
time: 146 us; the launch traced here: 145 us
  Pallas kernels  143 us (98%)
  between operations  1.95 us (1%)
    pallas_call x1, Pallas kernels, body(): pl.pallas_call(functools.partial(kernel, groups, blocks), out_shape=(jax....  142 us

profile of v6, /device:TPU:2, one launch (start us, length us, event | category | flops | bytes accessed | tf_op | source)
XLA Modules:
  0.0 145.5 jit_solution(16018130190289960940)
XLA Ops:
  1.3 0.0 copy-start
  1.9 0.0 copy-done
  2.0 142.3 %shard_map.76 = (bf16[384,1152]{1,0:T(8,128)(2,1)S(1)}, bf16[384,1152]{1,0:T(8,128)(2,1)S(1)}, f32[384]{0:T(512)S(1)}) custom-call(bf16[384,1152]{1,0:T(8,128)(2,1)} %image.1, bf16[384,1152]{1,0:T(8,128)(2,1)} %text.1, s32[1,384]{1,0:T(1,128)S(1)} %copy-done, f32[1]{0:T(128)} %bitcast.2.log_scale, f32[1]{0:T(128)} %bitcast.3.bias), custom_call_target="tpu_custom_call" | custom-call | tf_op jit(solution)/shard_map/pallas_call | solution.py:539
  144.2 1.2 shard_map.77
Async XLA Ops:
  1.3 0.7 copy-start
